TPU v7x, 32 devices: a whole 2x2x4 slice. The times are simulated.
32 devices in a mesh: lat: 4 (over y, x), lon: 8 (over z, core).
Axes of the slice: x: 2, y: 2, z: 4, core: 2. Of those that a mesh axis runs over, the one named last changes fastest.
Arguments:
- field: bfloat16 [128, 1024, 128], P('lat', 'lon'), may hold values from -60 to 60
- w_first: bfloat16 [3, 3, 128, 128], replicated, may hold values from -0.1875 to 0.1875
- w_down: bfloat16 [3, 3, 128, 256], replicated, may hold values from -0.1875 to 0.1875
- keep_first: int32 [128, 128], replicated, may hold values 0 or 1
- chan_first: int32 [128], replicated, may hold values 0 or 1
- keep_down: int32 [128, 256], replicated, may hold values 0 or 1
- chan_down: int32 [256], replicated, may hold values 0 or 1
- group_ids: int32 [128], replicated, may hold values from 0 to 31, as said below
- norm_gain: float32 [128], replicated, may hold values from 0.1 to 1.9
- norm_bias: float32 [128], replicated, may hold values from -3 to 3
Outputs:
- student_out: bfloat16 [64, 512, 256], P('lat', 'lon')
- grad_first: float32 [1152, 128], P(('lat', 'lon'))
- grad_down: float32 [1152, 256], P(('lat', 'lon'))
Inputs may be any that keep to these rules, and one draw needn't show every extreme that they name: `group_ids`: each of the 32 groups holds exactly 4 channels.
All inputs are finite; a program needn't handle non-finite values.
Results may differ from a plain program's by a relative error of at most 0.005.
Values may be sent and summed in bfloat16 or wider, within the bound.
A program may use at most 128 MiB of HBM per device.

v0:
```python
import functools

import jax
import jax.numpy as jnp
from jax import lax
from jax.experimental import pallas as pl
from jax.experimental.pallas import tpu as pltpu
from jax.sharding import PartitionSpec as P

GROUPS = 32
EPS = 1e-05
LOSS_WEIGHT = 64.0
MESH = pl.DeviceIdType.MESH
F32 = jnp.float32
BF16 = jnp.bfloat16
HIGH = lax.Precision.HIGHEST
BLOCK = 8


def dot(a, b):
    return jnp.dot(a, b, preferred_element_type=F32)


def kernel(
    nlat, nlon, chunk, padded,
    field, w_first, w_down, keep_first, chan_first, keep_down, chan_down, group_ids, gain_ref, bias_ref,
    out_ref, gfirst_ref, gdown_ref,
    ext, tmp, taps, pre, hid, hcol, hcol_in, hcorner, cot, ccol, ccol_in, ccorner, ghat, gturn, cturn,
    wf, wd, wt, gf, gd, send_f, send_d, got_f, got_d, stat_a, stat_b,
    own_sem, halo_s, halo_r, hid_s, hid_r, cot_s, cot_r, sa_s, sa_r, sb_s, sb_r, rf_s, rf_r, rd_s, rd_r,
):
    devices = nlat * nlon
    rows, cols, ch = field.shape
    out_ch = w_down.shape[3]
    half, wide = rows // 2, cols // 2
    lat, lon = lax.axis_index("lat"), lax.axis_index("lon")
    me = lat * nlon + lon
    west, east = lax.rem(lon + nlon - 1, nlon), lax.rem(lon + 1, nlon)
    has_up, has_down = lat > 0, lat < nlat - 1

    def place(index):
        return (index // nlon, lax.rem(index, nlon))

    own = pltpu.make_async_copy(field, ext.at[pl.ds(1, rows), pl.ds(16, cols)], own_sem)
    own.start()

    barrier = pltpu.get_barrier_semaphore()

    def greet(k, carry):
        pl.semaphore_signal(barrier, inc=1, device_id=place(lax.rem(me + k, devices)), device_id_type=MESH)
        return carry

    lax.fori_loop(1, devices, greet, 0)
    pl.semaphore_wait(barrier, devices - 1)

    def remote(src, dst, ssem, rsem, target):
        return pltpu.make_async_remote_copy(
            src_ref=src, dst_ref=dst, send_sem=ssem, recv_sem=rsem, device_id=target, device_id_type=MESH
        )

    def guarded(condition, action):
        if condition is None:
            action()
        else:
            pl.when(condition)(action)

    def begin(plans):
        for copy, sends, _ in plans:
            guarded(sends, copy.start)

    def finish_sends(plans):
        for copy, sends, _ in plans:
            guarded(sends, copy.wait_send)

    def finish_receives(plans):
        for copy, _, receives in plans:
            guarded(receives, copy.wait_recv)

    up, down = jnp.maximum(lat - 1, 0), jnp.minimum(lat + 1, nlat - 1)
    left, right, centre = pl.ds(0, 16), pl.ds(cols - 16, 16), pl.ds(16, cols)
    far = pl.ds(16 + cols, 16)
    first, last = pl.ds(0, 1), pl.ds(rows - 1, 1)
    below = pl.ds(rows + 1, 1)

    def halo(i, src, dst, target, sends, receives):
        return (remote(src, dst, halo_s.at[i], halo_r.at[i], target), sends, receives)

    halos = [
        halo(0, field.at[first], ext.at[below, centre], (up, lon), has_up, has_down),
        halo(1, field.at[last], ext.at[first, centre], (down, lon), has_down, has_up),
        halo(2, field.at[:, left], ext.at[pl.ds(1, rows), far], (lat, west), None, None),
        halo(3, field.at[:, right], ext.at[pl.ds(1, rows), left], (lat, east), None, None),
        halo(4, field.at[first, left], ext.at[below, far], (up, west), has_up, has_down),
        halo(5, field.at[first, right], ext.at[below, left], (up, east), has_up, has_down),
        halo(6, field.at[last, left], ext.at[first, far], (down, west), has_down, has_up),
        halo(7, field.at[last, right], ext.at[first, left], (down, east), has_down, has_up),
    ]
    begin(halos)

    @pl.when(jnp.logical_not(has_up))
    def _():
        ext[0] = jnp.zeros(ext.shape[1:], BF16)

    @pl.when(jnp.logical_not(has_down))
    def _():
        ext[rows + 1] = jnp.zeros(ext.shape[1:], BF16)

    mask_first = (keep_first[...] * chan_first[...]).astype(F32)
    mask_down = (keep_down[...] * chan_down[...]).astype(F32)
    for a in range(3):
        wt[a, out_ch:, :ch] = jnp.zeros((out_ch, ch), BF16)
        for b in range(3):
            here = slice(b * ch, (b + 1) * ch)
            wf[a, here, :ch] = w_first[a, b]
            wf[a, here, ch:] = (w_first[a, b].astype(F32) * mask_first).astype(BF16)
            student = w_down[a, b].astype(F32) * mask_down
            wd[0, a, here] = w_down[a, b]
            wd[1, a, here] = student.astype(BF16)
            turned = student.T.astype(BF16)
            if b == 0:
                wt[a, out_ch:, ch:] = turned
            elif b == 1:
                wt[a, :out_ch, :ch] = turned
            else:
                wt[a, :out_ch, ch:] = turned
    ids = jnp.broadcast_to(group_ids[...].astype(F32), (ch, ch))
    member = (ids == ids.T).astype(F32)
    gain, bias = gain_ref[...], bias_ref[...]

    own.wait()
    finish_receives(halos)

    def spread(r, carry):
        for e in range(2):
            tmp[e] = ext[2 * r + e].astype(F32)
            for k in range(4):
                taps[e, r, :, k * ch : (k + 1) * ch] = tmp[e, pl.ds(15 + k, wide, stride=2), :].astype(BF16)
        return carry

    lax.fori_loop(0, half + 1, spread, 0)

    size = BLOCK * wide
    total = jnp.zeros((1, 2 * ch), F32)
    for e in range(2):
        for p in range(2):

            def convolve(step, carry, e=e, p=p):
                r = step * BLOCK
                acc = None
                for a in range(3):
                    lhs = taps[(e + a) % 2, pl.ds(r + (e + a) // 2, BLOCK), :, p * ch : (p + 3) * ch]
                    part = dot(lhs.reshape(size, 3 * ch), wf[a])
                    acc = part if acc is None else acc + part
                pre[e, p, pl.ds(r, BLOCK)] = acc.reshape(BLOCK, wide, 2 * ch)
                return carry + jnp.sum(acc, axis=0, keepdims=True)

            total = lax.fori_loop(0, half // BLOCK, convolve, total)
    finish_sends(halos)

    def fold(value):
        return jnp.concatenate([value[:, :ch], value[:, ch:]], axis=0)

    cells = float(rows * cols)
    mean = total / cells

    def squares(r, carry):
        for e in range(2):
            for p in range(2):
                gap = pre[e, p, r] - mean
                carry = carry + jnp.sum(gap * gap, axis=0, keepdims=True)
        return carry

    spread_sum = lax.fori_loop(0, half, squares, jnp.zeros((1, 2 * ch), F32))

    def everyone(source, target, ssem, rsem):
        def start(k, carry):
            to = lax.rem(me + k, devices)
            remote(source(to), target.at[me], ssem.at[k], rsem.at[k], place(to)).start()
            return carry

        def receive(k, carry):
            at = lax.rem(me + devices - k, devices)
            remote(source(at), target.at[at], ssem.at[k], rsem.at[k], place(at)).wait_recv()
            return carry

        def sent(k, carry):
            to = lax.rem(me + k, devices)
            remote(source(to), target.at[me], ssem.at[k], rsem.at[k], place(to)).wait_send()
            return carry

        return (
            lambda: lax.fori_loop(1, devices, start, 0),
            lambda: lax.fori_loop(1, devices, receive, 0),
            lambda: lax.fori_loop(1, devices, sent, 0),
        )

    def grouped(value):
        return jnp.dot(value, member, precision=HIGH, preferred_element_type=F32)

    per_group = ch // GROUPS
    count = cells * devices * per_group
    stat_a[me] = jnp.concatenate([fold(mean), fold(spread_sum), jnp.zeros((4, ch), F32)], axis=0)
    go, receive, sent_a = everyone(lambda to: stat_a.at[me], stat_a, sa_s, sa_r)
    go()
    receive()
    stats = stat_a[...]
    centre8 = grouped(jnp.sum(stats, axis=0)) / float(devices * per_group)
    centre2 = centre8[0:2]
    drift = stats[:, 0:2] - centre2[None]
    moment = jnp.sum(stats[:, 2:4] + cells * (drift * drift), axis=0)
    variance = grouped(jnp.concatenate([moment, jnp.zeros((6, ch), F32)], axis=0))[0:2] / count
    inv2 = lax.rsqrt(variance + EPS)
    centre_s, inv_s = centre2[1:2], inv2[1:2]
    centre_both = jnp.concatenate([centre2[0:1], centre_s], axis=1)
    inv_both = jnp.concatenate([inv2[0:1], inv_s], axis=1)
    gain_both = jnp.concatenate([gain, gain], axis=1)
    bias_both = jnp.concatenate([bias, bias], axis=1)

    def activate(r, carry):
        for e in range(2):
            at = r + 1 if e else r + half + 1
            for p in range(2):
                normed = (pre[e, p, r] - centre_both) * inv_both * gain_both + bias_both
                value = normed * jax.nn.sigmoid(normed)
                rounded = value.astype(BF16)
                for net in range(2):
                    hid[net, at, :, (p + 1) * ch : (p + 2) * ch] = rounded[:, net * ch : (net + 1) * ch]
                if p:
                    value = rounded.astype(F32)
                    hcol[pl.ds(e * half + r, 1), :] = value[wide - 1 :, :]
                    rolled = pltpu.roll(value, 1, 0).astype(BF16)
                    for net in range(2):
                        hid[net, at, :, :ch] = rolled[:, net * ch : (net + 1) * ch]
        return carry

    lax.fori_loop(0, half, activate, 0)
    hids = [
        (remote(hid.at[:, half], hid.at[:, 0], hid_s.at[0], hid_r.at[0], (down, lon)), has_down, has_up),
        (remote(hcol, hcol_in, hid_s.at[1], hid_r.at[1], (lat, east)), None, None),
        (remote(hcol.at[pl.ds(rows - 8, 8)], hcorner, hid_s.at[2], hid_r.at[2], (down, east)), has_down, has_up),
    ]
    begin(hids)
    sent_a()

    @pl.when(jnp.logical_not(has_up))
    def _():
        hid[:, 0] = jnp.zeros((2, wide, 3 * ch), BF16)
        hcorner[...] = jnp.zeros(hcorner.shape, F32)

    finish_sends(hids)
    finish_receives(hids)
    top = lax.broadcasted_iota(jnp.int32, (16, ch), 0) == 0

    def put_west(at, value):
        for net in range(2):
            tile = hid[net, at, :16, :ch].astype(F32)
            new = jnp.broadcast_to(value[:, net * ch : (net + 1) * ch], (16, ch))
            hid[net, at, :16, :ch] = jnp.where(top, new, tile).astype(BF16)

    def mend(r, carry):
        put_west(r + half + 1, hcol_in[pl.ds(r, 1), :])
        put_west(r + 1, hcol_in[pl.ds(r + half, 1), :])
        return carry

    lax.fori_loop(0, half, mend, 0)
    put_west(0, hcorner[7:8, :])

    starts = (0, half + 1, 1)
    scale = LOSS_WEIGHT / float(half * wide * devices)

    def shrink(step, carry):
        r = step * BLOCK
        both = []
        for net in range(2):
            acc = None
            for a in range(3):
                lhs = hid[net, pl.ds(r + starts[a], BLOCK)].reshape(size, 3 * ch)
                part = dot(lhs, wd[net, a])
                acc = part if acc is None else acc + part
            both.append(acc)
        out_ref[pl.ds(r, BLOCK)] = both[1].astype(BF16).reshape(BLOCK, wide, out_ch)
        ct = (scale * (both[1] - both[0])).astype(BF16)
        cot[pl.ds(r, BLOCK), :, :out_ch] = ct.reshape(BLOCK, wide, out_ch)
        ct32 = ct.astype(F32)
        for q in range(BLOCK):
            line = ct32[q * wide : (q + 1) * wide]
            ccol[pl.ds(r + q, 1), :] = line[0:1]
            cot[r + q, :, out_ch:] = pltpu.roll(line, wide - 1, 0).astype(BF16)
        return carry

    lax.fori_loop(0, half // BLOCK, shrink, 0)
    cots = [
        (remote(cot.at[0], cot.at[half], cot_s.at[0], cot_r.at[0], (up, lon)), has_up, has_down),
        (remote(ccol, ccol_in, cot_s.at[1], cot_r.at[1], (lat, west)), None, None),
        (remote(ccol.at[pl.ds(0, 8)], ccorner, cot_s.at[2], cot_r.at[2], (up, west)), has_up, has_down),
    ]
    begin(cots)

    @pl.when(jnp.logical_not(has_down))
    def _():
        cot[half] = jnp.zeros((wide, 2 * out_ch), BF16)
        ccorner[...] = jnp.zeros(ccorner.shape, F32)

    for step in range(half // BLOCK):
        piece = cot[step * BLOCK : (step + 1) * BLOCK, :, :out_ch].reshape(size, out_ch)
        cturn[:, step * size : (step + 1) * size] = piece.astype(F32).T.astype(BF16)
    finish_sends(cots)
    finish_receives(cots)
    bottom = lax.broadcasted_iota(jnp.int32, (16, out_ch), 0) == 15

    def put_east(at, value):
        tile = cot[at, wide - 16 :, out_ch:].astype(F32)
        cot[at, wide - 16 :, out_ch:] = jnp.where(bottom, jnp.broadcast_to(value, (16, out_ch)), tile).astype(BF16)

    def mend_east(r, carry):
        put_east(r, ccol_in[pl.ds(r, 1), :])
        return carry

    lax.fori_loop(0, half, mend_east, 0)
    put_east(half, ccorner[0:1, :])

    def backward(step, carry):
        r = step * BLOCK
        here = cot[pl.ds(r, BLOCK)].reshape(size, 2 * out_ch)
        after = cot[pl.ds(r + 1, BLOCK)].reshape(size, 2 * out_ch)
        pair = (dot(here, wt[1]), dot(here, wt[2]) + dot(after, wt[0]))
        one, two = carry
        for e in range(2):
            for p in range(2):
                hat = (pre[e, p, pl.ds(r, BLOCK), :, ch:].reshape(size, ch) - centre_s) * inv_s
                normed = hat * gain + bias
                sigma = jax.nn.sigmoid(normed)
                value = pair[e][:, p * ch : (p + 1) * ch] * sigma * (1.0 + normed * (1.0 - sigma)) * gain
                ghat[e, pl.ds(r, BLOCK), :, p * ch : (p + 1) * ch] = value.reshape(BLOCK, wide, ch)
                one = one + jnp.sum(value, axis=0, keepdims=True)
                two = two + jnp.sum(value * hat, axis=0, keepdims=True)
        return one, two

    zero = jnp.zeros((1, ch), F32)
    one, two = lax.fori_loop(0, half // BLOCK, backward, (zero, zero))
    stat_b[me] = jnp.concatenate([one, two, jnp.zeros((6, ch), F32)], axis=0)
    go, receive_b, sent_b = everyone(lambda to: stat_b.at[me], stat_b, sb_s, sb_r)
    go()

    def pack(grads, buffer):
        for d in range(devices):
            buffer[d] = grads[d * chunk : d * chunk + padded, :].astype(BF16)

    gd[9 * ch :, :] = jnp.zeros((16, out_ch), F32)
    gf[9 * ch :, :] = jnp.zeros((16, ch), F32)
    for a in range(3):
        turned = dot(cturn[...], hid[1, starts[a] : starts[a] + half].reshape(half * wide, 3 * ch))
        for b in range(3):
            at = (a * 3 + b) * ch
            gd[at : at + ch, :] = turned[:, b * ch : (b + 1) * ch].T * mask_down
    pack(gd, send_d)
    go_d, receive_d, sent_d = everyone(lambda to: send_d.at[to], got_d, rd_s, rd_r)
    go_d()
    got_d[me] = send_d[me]

    receive_b()
    back = grouped(jnp.sum(stat_b[...], axis=0)) / count
    m1, m2 = back[0:1], back[1:2]
    for e in range(2):
        for step in range(half // BLOCK):
            r = step * BLOCK
            for p in range(2):
                hat = (pre[e, p, r : r + BLOCK, :, ch:].reshape(size, ch) - centre_s) * inv_s
                value = ghat[e, r : r + BLOCK, :, p * ch : (p + 1) * ch].reshape(size, ch)
                gpre = inv_s * (value - m1 - hat * m2)
                gturn[e, p * ch : (p + 1) * ch, step * size : (step + 1) * size] = gpre.T.astype(BF16)
    for a in range(3):
        acc = None
        for e in range(2):
            start = (e + a) // 2
            part = dot(gturn[e], taps[(e + a) % 2, start : start + half].reshape(half * wide, 4 * ch))
            acc = part if acc is None else acc + part
        for b in range(3):
            at = (a * 3 + b) * ch
            block = acc[:ch, b * ch : (b + 1) * ch] + acc[ch:, (b + 1) * ch : (b + 2) * ch]
            gf[at : at + ch, :] = block.T * mask_first
    pack(gf, send_f)
    go_f, receive_f, sent_f = everyone(lambda to: send_f.at[to], got_f, rf_s, rf_r)
    go_f()
    got_f[me] = send_f[me]

    def add_up(got, width):
        def add(d, acc):
            return acc + got[d].astype(F32)

        return lax.fori_loop(0, devices, add, jnp.zeros((padded, width), F32))[:chunk]

    receive_d()
    gdown_ref[...] = add_up(got_d, out_ch)
    receive_f()
    gfirst_ref[...] = add_up(got_f, ch)
    sent_b()
    sent_d()
    sent_f()


def local(nlat, nlon, field, w_first, w_down, keep_first, chan_first, keep_down, chan_down, group_ids, norm_gain, norm_bias):
    rows, cols, ch = field.shape
    out_ch = w_down.shape[3]
    devices = nlat * nlon
    half, wide = rows // 2, cols // 2
    chunk = 9 * ch // devices
    padded = -(-chunk // 16) * 16
    vmem = pl.BlockSpec(memory_space=pltpu.VMEM)
    dma = pltpu.SemaphoreType.DMA
    S = pltpu.VMEM
    return tuple(
        pl.pallas_call(
            functools.partial(kernel, nlat, nlon, chunk, padded),
            out_shape=(
                jax.ShapeDtypeStruct((half, wide, out_ch), BF16),
                jax.ShapeDtypeStruct((chunk, ch), F32),
                jax.ShapeDtypeStruct((chunk, out_ch), F32),
            ),
            in_specs=[pl.BlockSpec(memory_space=pl.ANY)] + [vmem] * 9,
            out_specs=(vmem, vmem, vmem),
            scratch_shapes=[
                S((rows + 2, cols + 32, ch), BF16),
                S((2, cols + 32, ch), F32),
                S((2, half + 1, wide, 4 * ch), BF16),
                S((2, 2, half, wide, 2 * ch), F32),
                S((2, rows + 1, wide, 3 * ch), BF16),
                S((rows, 2 * ch), F32),
                S((rows, 2 * ch), F32),
                S((8, 2 * ch), F32),
                S((half + 1, wide, 2 * out_ch), BF16),
                S((half, out_ch), F32),
                S((half, out_ch), F32),
                S((8, out_ch), F32),
                S((2, half, wide, 2 * ch), F32),
                S((2, 2 * ch, half * wide), BF16),
                S((out_ch, half * wide), BF16),
                S((3, 3 * ch, 2 * ch), BF16),
                S((2, 3, 3 * ch, out_ch), BF16),
                S((3, 2 * out_ch, 2 * ch), BF16),
                S((9 * ch + 16, ch), F32),
                S((9 * ch + 16, out_ch), F32),
                S((devices, padded, ch), BF16),
                S((devices, padded, out_ch), BF16),
                S((devices, padded, ch), BF16),
                S((devices, padded, out_ch), BF16),
                S((devices, 8, ch), F32),
                S((devices, 8, ch), F32),
                dma,
                dma((8,)), dma((8,)),
                dma((3,)), dma((3,)),
                dma((3,)), dma((3,)),
                dma((devices,)), dma((devices,)),
                dma((devices,)), dma((devices,)),
                dma((devices,)), dma((devices,)),
                dma((devices,)), dma((devices,)),
            ],
            compiler_params=pltpu.CompilerParams(
                collective_id=0, has_side_effects=True, vmem_limit_bytes=56 * 1024 * 1024
            ),
        )(
            field,
            w_first,
            w_down,
            keep_first,
            chan_first.reshape(1, ch),
            keep_down,
            chan_down.reshape(1, out_ch),
            group_ids.reshape(1, ch),
            norm_gain.reshape(1, ch),
            norm_bias.reshape(1, ch),
        )
    )


def solution(mesh):
    return jax.shard_map(
        functools.partial(local, mesh.shape["lat"], mesh.shape["lon"]),
        mesh=mesh,
        in_specs=(P("lat", "lon", None), P(), P(), P(), P(), P(), P(), P(), P(), P()),
        out_specs=(P("lat", "lon", None), P(("lat", "lon"), None), P(("lat", "lon"), None)),
        check_vma=False,
    )
```

profile of v0, /device:TPU:0, one launch (start us, length us, event | category | flops | bytes accessed | tf_op | source)
XLA Modules:
  0.0 76.9 jit_solution(7824491958323765066)
XLA Ops:
  0.6 73.0 %shard_map.121 = (bf16[16,64,256]{2,1,0:T(8,128)(2,1)}, f32[36,128]{1,0:T(8,128)}, f32[36,256]{1,0:T(8,128)}) custom-call(bf16[32,128,128]{2,1,0:T(8,128)(2,1)} %field.1, bf16[3,3,128,128]{3,2,1,0:T(8,128)(2,1)} %w_first.1, bf16[3,3,128,256]{3,2,1,0:T(8,128)(2,1)} %w_down.1, s32[128,128]{1,0:T(8,128)} %keep_first.1, s32[1,128]{1,0:T(1,128)} %bitcast.6, ...), custom_call_target="tpu_custom_call" | custom-call | tf_op jit(solution)/shard_map/pallas_call | solution.py:413
  73.6 0.0 copy-start.1
  73.6 1.9 %copy.16 = bf16[16,64,256]{2,1,0:T(8,128)(2,1)} copy(bf16[16,64,256]{2,1,0:T(8,128)(2,1)} %get-tuple-element.6) | data formatting | bytes 1048576
  75.5 0.0 copy-done.1
  75.5 0.0 copy-start
  75.5 0.6 copy.17
  76.1 0.2 copy-done
  76.3 0.6 copy.18
Async XLA Ops:
  73.6 1.9 %copy-start.1 = (f32[36,128]{1,0:T(8,128)S(1)}, f32[36,128]{1,0:T(8,128)}, u32[]{:S(2)}) copy-start(f32[36,128]{1,0:T(8,128)} %get-tuple-element.7) | copy-start | bytes 55300
  75.5 0.8 %copy-start = (f32[36,256]{1,0:T(8,128)S(1)}, f32[36,256]{1,0:T(8,128)}, u32[]{:S(2)}) copy-start(f32[36,256]{1,0:T(8,128)} %get-tuple-element.8) | copy-start | bytes 110596
where the time goes:
time: 77.1 us; the launch traced here: 76.9 us
  Pallas kernels  73 us (95%)
  local copies, waits for them, and re-layouts  3.29 us (4%)
    pallas_call x1, Pallas kernels, local(): pl.pallas_call(functools.partial(kernel, nlat, nlon, chunk, padded), out_...  73 us
    unnamed x7, local copies, waits for them, and re-layouts  3.29 us

commit v1 on v0

--- a/solution.py
+++ b/solution.py
@@ -26,8 +26,8 @@
     field, w_first, w_down, keep_first, chan_first, keep_down, chan_down, group_ids, gain_ref, bias_ref,
     out_ref, gfirst_ref, gdown_ref,
     ext, tmp, taps, pre, hid, hcol, hcol_in, hcorner, cot, ccol, ccol_in, ccorner, ghat, gturn, cturn,
-    wf, wd, wt, gf, gd, send_f, send_d, got_f, got_d, stat_a, stat_b,
-    own_sem, halo_s, halo_r, hid_s, hid_r, cot_s, cot_r, sa_s, sa_r, sb_s, sb_r, rf_s, rf_r, rd_s, rd_r,
+    wf, wd, wt, gf, gd, send_f, send_d, other_f, other_d, merged_f, merged_d, got_f, got_d, stat_a, stat_b,
+    own_sem, halo_s, halo_r, hid_s, hid_r, cot_s, cot_r, sa_s, sa_r, sb_s, sb_r, swap_s, swap_r, rf_s, rf_r, rd_s, rd_r,
 ):
     devices = nlat * nlon
     rows, cols, ch = field.shape
@@ -342,9 +342,47 @@
     go, receive_b, sent_b = everyone(lambda to: stat_b.at[me], stat_b, sb_s, sb_r)
     go()
 
+    pairs = devices // 2
+    core = lax.rem(lon, 2)
+    mine = me // 2
+    mate = (lat, lon + 1 - 2 * core)
+
     def pack(grads, buffer):
         for d in range(devices):
-            buffer[d] = grads[d * chunk : d * chunk + padded, :].astype(BF16)
+            buffer[d % 2, d // 2] = grads[d * chunk : d * chunk + padded, :].astype(BF16)
+
+    def merge(buffer, other, merged, got):
+        def one_chunk(h, carry):
+            merged[h] = (buffer[core, h].astype(F32) + other[h].astype(F32)).astype(BF16)
+            return carry
+
+        lax.fori_loop(0, pairs, one_chunk, 0)
+        got[mine] = merged[mine]
+
+    def scatter(merged, got, ssem, rsem):
+        def owner(h):
+            return place(2 * h + core)
+
+        def start(k, carry):
+            to = lax.rem(mine + k, pairs)
+            remote(merged.at[to], got.at[mine], ssem.at[k], rsem.at[k], owner(to)).start()
+            return carry
+
+        def receive(k, carry):
+            at = lax.rem(mine + pairs - k, pairs)
+            remote(merged.at[at], got.at[at], ssem.at[k], rsem.at[k], owner(at)).wait_recv()
+            return carry
+
+        def sent(k, carry):
+            to = lax.rem(mine + k, pairs)
+            remote(merged.at[to], got.at[mine], ssem.at[k], rsem.at[k], owner(to)).wait_send()
+            return carry
+
+        return (
+            lambda: lax.fori_loop(1, pairs, start, 0),
+            lambda: lax.fori_loop(1, pairs, receive, 0),
+            lambda: lax.fori_loop(1, pairs, sent, 0),
+        )
 
     gd[9 * ch :, :] = jnp.zeros((16, out_ch), F32)
     gf[9 * ch :, :] = jnp.zeros((16, ch), F32)
@@ -354,9 +392,9 @@
             at = (a * 3 + b) * ch
             gd[at : at + ch, :] = turned[:, b * ch : (b + 1) * ch].T * mask_down
     pack(gd, send_d)
-    go_d, receive_d, sent_d = everyone(lambda to: send_d.at[to], got_d, rd_s, rd_r)
-    go_d()
-    got_d[me] = send_d[me]
+    swap_d = remote(send_d.at[1 - core], other_d, swap_s.at[0], swap_r.at[0], mate)
+    swap_d.start()
+    go_d, receive_d, sent_d = scatter(merged_d, got_d, rd_s, rd_r)
 
     receive_b()
     back = grouped(jnp.sum(stat_b[...], axis=0)) / count
@@ -369,6 +407,9 @@
                 value = ghat[e, r : r + BLOCK, :, p * ch : (p + 1) * ch].reshape(size, ch)
                 gpre = inv_s * (value - m1 - hat * m2)
                 gturn[e, p * ch : (p + 1) * ch, step * size : (step + 1) * size] = gpre.T.astype(BF16)
+    swap_d.wait_recv()
+    merge(send_d, other_d, merged_d, got_d)
+    go_d()
     for a in range(3):
         acc = None
         for e in range(2):
@@ -380,16 +421,19 @@
             block = acc[:ch, b * ch : (b + 1) * ch] + acc[ch:, (b + 1) * ch : (b + 2) * ch]
             gf[at : at + ch, :] = block.T * mask_first
     pack(gf, send_f)
-    go_f, receive_f, sent_f = everyone(lambda to: send_f.at[to], got_f, rf_s, rf_r)
-    go_f()
-    got_f[me] = send_f[me]
+    swap_f = remote(send_f.at[1 - core], other_f, swap_s.at[1], swap_r.at[1], mate)
+    swap_f.start()
+    go_f, receive_f, sent_f = scatter(merged_f, got_f, rf_s, rf_r)
 
     def add_up(got, width):
         def add(d, acc):
             return acc + got[d].astype(F32)
 
-        return lax.fori_loop(0, devices, add, jnp.zeros((padded, width), F32))[:chunk]
-
+        return lax.fori_loop(0, pairs, add, jnp.zeros((padded, width), F32))[:chunk]
+
+    swap_f.wait_recv()
+    merge(send_f, other_f, merged_f, got_f)
+    go_f()
     receive_d()
     gdown_ref[...] = add_up(got_d, out_ch)
     receive_f()
@@ -397,12 +441,15 @@
     sent_b()
     sent_d()
     sent_f()
+    swap_d.wait_send()
+    swap_f.wait_send()
 
 
 def local(nlat, nlon, field, w_first, w_down, keep_first, chan_first, keep_down, chan_down, group_ids, norm_gain, norm_bias):
     rows, cols, ch = field.shape
     out_ch = w_down.shape[3]
     devices = nlat * nlon
+    pairs = devices // 2
     half, wide = rows // 2, cols // 2
     chunk = 9 * ch // devices
     padded = -(-chunk // 16) * 16
@@ -440,10 +487,14 @@
                 S((3, 2 * out_ch, 2 * ch), BF16),
                 S((9 * ch + 16, ch), F32),
                 S((9 * ch + 16, out_ch), F32),
-                S((devices, padded, ch), BF16),
-                S((devices, padded, out_ch), BF16),
-                S((devices, padded, ch), BF16),
-                S((devices, padded, out_ch), BF16),
+                S((2, pairs, padded, ch), BF16),
+                S((2, pairs, padded, out_ch), BF16),
+                S((pairs, padded, ch), BF16),
+                S((pairs, padded, out_ch), BF16),
+                S((pairs, padded, ch), BF16),
+                S((pairs, padded, out_ch), BF16),
+                S((pairs, padded, ch), BF16),
+                S((pairs, padded, out_ch), BF16),
                 S((devices, 8, ch), F32),
                 S((devices, 8, ch), F32),
                 dma,
@@ -452,8 +503,9 @@
                 dma((3,)), dma((3,)),
                 dma((devices,)), dma((devices,)),
                 dma((devices,)), dma((devices,)),
-                dma((devices,)), dma((devices,)),
-                dma((devices,)), dma((devices,)),
+                dma((2,)), dma((2,)),
+                dma((pairs,)), dma((pairs,)),
+                dma((pairs,)), dma((pairs,)),
             ],
             compiler_params=pltpu.CompilerParams(
                 collective_id=0, has_side_effects=True, vmem_limit_bytes=56 * 1024 * 1024

time: 77.1 us -> 67.7 us (0.88)
  Pallas kernels: 73 us -> 63.5 us
    pallas_call x1, Pallas kernels: 73 us -> 63.5 us  [local(): pl.pallas_call(functools.partial(kernel, nlat, nlon, chunk, padded), out_...]
where the time goes in v1:
time: 67.7 us; the launch traced here: 67.5 us
  Pallas kernels  63.5 us (94%)
  local copies, waits for them, and re-layouts  3.29 us (5%)
    pallas_call x1, Pallas kernels, local(): pl.pallas_call(functools.partial(kernel, nlat, nlon, chunk, padded), out_...  63.5 us
    unnamed x7, local copies, waits for them, and re-layouts  3.29 us

profile of v1, /device:TPU:0, one launch (start us, length us, event | category | flops | bytes accessed | tf_op | source)
XLA Modules:
  0.0 67.5 jit_solution(8841266167564451024)
XLA Ops:
  0.6 63.5 %shard_map.121 = (bf16[16,64,256]{2,1,0:T(8,128)(2,1)}, f32[36,128]{1,0:T(8,128)}, f32[36,256]{1,0:T(8,128)}) custom-call(bf16[32,128,128]{2,1,0:T(8,128)(2,1)} %field.1, bf16[3,3,128,128]{3,2,1,0:T(8,128)(2,1)} %w_first.1, bf16[3,3,128,256]{3,2,1,0:T(8,128)(2,1)} %w_down.1, s32[128,128]{1,0:T(8,128)} %keep_first.1, s32[1,128]{1,0:T(1,128)} %bitcast.6, ...), custom_call_target="tpu_custom_call" | custom-call | tf_op jit(solution)/shard_map/pallas_call | solution.py:460
  64.2 0.0 copy-start.1
  64.2 1.9 %copy.16 = bf16[16,64,256]{2,1,0:T(8,128)(2,1)} copy(bf16[16,64,256]{2,1,0:T(8,128)(2,1)} %get-tuple-element.6) | data formatting | bytes 1048576
  66.1 0.0 copy-done.1
  66.1 0.0 copy-start
  66.1 0.6 copy.17
  66.7 0.2 copy-done
  66.9 0.6 copy.18
Async XLA Ops:
  64.2 1.9 %copy-start.1 = (f32[36,128]{1,0:T(8,128)S(1)}, f32[36,128]{1,0:T(8,128)}, u32[]{:S(2)}) copy-start(f32[36,128]{1,0:T(8,128)} %get-tuple-element.7) | copy-start | bytes 55300
  66.1 0.8 %copy-start = (f32[36,256]{1,0:T(8,128)S(1)}, f32[36,256]{1,0:T(8,128)}, u32[]{:S(2)}) copy-start(f32[36,256]{1,0:T(8,128)} %get-tuple-element.8) | copy-start | bytes 110596

commit v2 on v1

--- a/solution.py
+++ b/solution.py
@@ -25,7 +25,7 @@
     nlat, nlon, chunk, padded,
     field, w_first, w_down, keep_first, chan_first, keep_down, chan_down, group_ids, gain_ref, bias_ref,
     out_ref, gfirst_ref, gdown_ref,
-    ext, tmp, taps, pre, hid, hcol, hcol_in, hcorner, cot, ccol, ccol_in, ccorner, ghat, gturn, cturn,
+    ext, tmp, taps, pre, hid, hcol, hcol_in, hcorner, hrow_in, outs, edge, cot, ccol, ccol_in, ccorner, ghat, gturn, cturn,
     wf, wd, wt, gf, gd, send_f, send_d, other_f, other_d, merged_f, merged_d, got_f, got_d, stat_a, stat_b,
     own_sem, halo_s, halo_r, hid_s, hid_r, cot_s, cot_r, sa_s, sa_r, sb_s, sb_r, swap_s, swap_r, rf_s, rf_r, rd_s, rd_r,
 ):
@@ -127,17 +127,39 @@
     member = (ids == ids.T).astype(F32)
     gain, bias = gain_ref[...], bias_ref[...]
 
+    top = lax.broadcasted_iota(jnp.int32, (16, ch), 0) == 0
+    foot = lax.broadcasted_iota(jnp.int32, (16, ch), 0) == 15
+    tmp[...] = jnp.zeros(tmp.shape, F32)
+
+    def spread_row(e, r, at):
+        tmp[e, 16 : 16 + cols] = ext[at, 16 : 16 + cols].astype(F32)
+        for k in range(4):
+            taps[e, r, :, k * ch : (k + 1) * ch] = tmp[e, pl.ds(15 + k, wide, stride=2), :].astype(BF16)
+
+    def mend_row(e, r, at):
+        before = pltpu.roll(ext[at, :16].astype(F32), 1, 0)
+        after = pltpu.roll(ext[at, 16 + cols :].astype(F32), 15, 0)
+        head = taps[e, r, :16, :ch].astype(F32)
+        tail = taps[e, r, wide - 16 :, 3 * ch :].astype(F32)
+        taps[e, r, :16, :ch] = jnp.where(top, before, head).astype(BF16)
+        taps[e, r, wide - 16 :, 3 * ch :] = jnp.where(foot, after, tail).astype(BF16)
+
+    def spread(r, carry):
+        spread_row(1, r, 2 * r + 1)
+        spread_row(0, r + 1, 2 * r + 2)
+        return carry
+
+    def mend_field(r, carry):
+        mend_row(0, r, 2 * r)
+        mend_row(1, r, 2 * r + 1)
+        return carry
+
     own.wait()
+    lax.fori_loop(0, half, spread, 0)
     finish_receives(halos)
-
-    def spread(r, carry):
-        for e in range(2):
-            tmp[e] = ext[2 * r + e].astype(F32)
-            for k in range(4):
-                taps[e, r, :, k * ch : (k + 1) * ch] = tmp[e, pl.ds(15 + k, wide, stride=2), :].astype(BF16)
-        return carry
-
-    lax.fori_loop(0, half + 1, spread, 0)
+    spread_row(0, 0, 0)
+    spread_row(1, half, rows + 1)
+    lax.fori_loop(0, half + 1, mend_field, 0)
 
     size = BLOCK * wide
     total = jnp.zeros((1, 2 * ch), F32)
@@ -216,6 +238,8 @@
     gain_both = jnp.concatenate([gain, gain], axis=1)
     bias_both = jnp.concatenate([bias, bias], axis=1)
 
+    crest = lax.broadcasted_iota(jnp.int32, (wide, 2 * ch), 0) == 0
+
     def activate(r, carry):
         for e in range(2):
             at = r + 1 if e else r + half + 1
@@ -228,14 +252,14 @@
                 if p:
                     value = rounded.astype(F32)
                     hcol[pl.ds(e * half + r, 1), :] = value[wide - 1 :, :]
-                    rolled = pltpu.roll(value, 1, 0).astype(BF16)
+                    rolled = jnp.where(crest, 0.0, pltpu.roll(value, 1, 0)).astype(BF16)
                     for net in range(2):
                         hid[net, at, :, :ch] = rolled[:, net * ch : (net + 1) * ch]
         return carry
 
     lax.fori_loop(0, half, activate, 0)
     hids = [
-        (remote(hid.at[:, half], hid.at[:, 0], hid_s.at[0], hid_r.at[0], (down, lon)), has_down, has_up),
+        (remote(hid.at[:, half], hrow_in, hid_s.at[0], hid_r.at[0], (down, lon)), has_down, has_up),
         (remote(hcol, hcol_in, hid_s.at[1], hid_r.at[1], (lat, east)), None, None),
         (remote(hcol.at[pl.ds(rows - 8, 8)], hcorner, hid_s.at[2], hid_r.at[2], (down, east)), has_down, has_up),
     ]
@@ -244,51 +268,54 @@
 
     @pl.when(jnp.logical_not(has_up))
     def _():
-        hid[:, 0] = jnp.zeros((2, wide, 3 * ch), BF16)
+        hrow_in[...] = jnp.zeros(hrow_in.shape, BF16)
         hcorner[...] = jnp.zeros(hcorner.shape, F32)
 
-    finish_sends(hids)
-    finish_receives(hids)
-    top = lax.broadcasted_iota(jnp.int32, (16, ch), 0) == 0
-
-    def put_west(at, value):
-        for net in range(2):
-            tile = hid[net, at, :16, :ch].astype(F32)
-            new = jnp.broadcast_to(value[:, net * ch : (net + 1) * ch], (16, ch))
-            hid[net, at, :16, :ch] = jnp.where(top, new, tile).astype(BF16)
-
-    def mend(r, carry):
-        put_west(r + half + 1, hcol_in[pl.ds(r, 1), :])
-        put_west(r + 1, hcol_in[pl.ds(r + half, 1), :])
-        return carry
-
-    lax.fori_loop(0, half, mend, 0)
-    put_west(0, hcorner[7:8, :])
-
+    hid[:, 0] = jnp.zeros((2, wide, 3 * ch), BF16)
     starts = (0, half + 1, 1)
     scale = LOSS_WEIGHT / float(half * wide * devices)
 
     def shrink(step, carry):
         r = step * BLOCK
-        both = []
         for net in range(2):
             acc = None
             for a in range(3):
                 lhs = hid[net, pl.ds(r + starts[a], BLOCK)].reshape(size, 3 * ch)
                 part = dot(lhs, wd[net, a])
                 acc = part if acc is None else acc + part
-            both.append(acc)
-        out_ref[pl.ds(r, BLOCK)] = both[1].astype(BF16).reshape(BLOCK, wide, out_ch)
+            outs[net, pl.ds(r, BLOCK)] = acc.reshape(BLOCK, wide, out_ch)
+        return carry
+
+    lax.fori_loop(0, half // BLOCK, shrink, 0)
+    finish_sends(hids)
+    finish_receives(hids)
+    west_even, west_odd = hcol_in[:half, :], hcol_in[half:, :]
+    west_last = jnp.concatenate([hcorner[7:8, :], west_odd[: half - 1]], axis=0)
+    for net in range(2):
+        here = slice(net * ch, (net + 1) * ch)
+        acc = dot(hrow_in[net], wd[net, 0])
+        outs[net, 0] = outs[net, 0] + acc
+        acc = None
+        for a, value in enumerate((west_last, west_even, west_odd)):
+            part = dot(value[:, here].astype(BF16), wd[net, a, :ch])
+            acc = part if acc is None else acc + part
+        edge[net] = acc
+    start_col = lax.broadcasted_iota(jnp.int32, (wide, out_ch), 0) == 0
+
+    def finish_row(r, carry):
+        both = []
+        for net in range(2):
+            extra = jnp.broadcast_to(edge[net, pl.ds(r, 1), :], (wide, out_ch))
+            both.append(outs[net, r] + jnp.where(start_col, extra, 0.0))
+        out_ref[r] = both[1].astype(BF16)
         ct = (scale * (both[1] - both[0])).astype(BF16)
-        cot[pl.ds(r, BLOCK), :, :out_ch] = ct.reshape(BLOCK, wide, out_ch)
-        ct32 = ct.astype(F32)
-        for q in range(BLOCK):
-            line = ct32[q * wide : (q + 1) * wide]
-            ccol[pl.ds(r + q, 1), :] = line[0:1]
-            cot[r + q, :, out_ch:] = pltpu.roll(line, wide - 1, 0).astype(BF16)
-        return carry
-
-    lax.fori_loop(0, half // BLOCK, shrink, 0)
+        cot[r, :, :out_ch] = ct
+        line = ct.astype(F32)
+        ccol[pl.ds(r, 1), :] = line[0:1]
+        cot[r, :, out_ch:] = pltpu.roll(line, wide - 1, 0).astype(BF16)
+        return carry
+
+    lax.fori_loop(0, half, finish_row, 0)
     cots = [
         (remote(cot.at[0], cot.at[half], cot_s.at[0], cot_r.at[0], (up, lon)), has_up, has_down),
         (remote(ccol, ccol_in, cot_s.at[1], cot_r.at[1], (lat, west)), None, None),
@@ -304,6 +331,26 @@
     for step in range(half // BLOCK):
         piece = cot[step * BLOCK : (step + 1) * BLOCK, :, :out_ch].reshape(size, out_ch)
         cturn[:, step * size : (step + 1) * size] = piece.astype(F32).T.astype(BF16)
+    def put_west(at, value):
+        tile = hid[1, at, :16, :ch].astype(F32)
+        new = jnp.broadcast_to(value[:, ch:], (16, ch))
+        hid[1, at, :16, :ch] = jnp.where(top, new, tile).astype(BF16)
+
+    def mend(r, carry):
+        put_west(r + half + 1, hcol_in[pl.ds(r, 1), :])
+        put_west(r + 1, hcol_in[pl.ds(r + half, 1), :])
+        return carry
+
+    hid[1, 0] = hrow_in[1]
+    lax.fori_loop(0, half, mend, 0)
+    put_west(0, hcorner[7:8, :])
+    gd[9 * ch :, :] = jnp.zeros((16, out_ch), F32)
+    gf[9 * ch :, :] = jnp.zeros((16, ch), F32)
+    for a in range(3):
+        turned = dot(cturn[...], hid[1, starts[a] : starts[a] + half].reshape(half * wide, 3 * ch))
+        for b in range(3):
+            at = (a * 3 + b) * ch
+            gd[at : at + ch, :] = turned[:, b * ch : (b + 1) * ch].T * mask_down
     finish_sends(cots)
     finish_receives(cots)
     bottom = lax.broadcasted_iota(jnp.int32, (16, out_ch), 0) == 15
@@ -384,13 +431,6 @@
             lambda: lax.fori_loop(1, pairs, sent, 0),
         )
 
-    gd[9 * ch :, :] = jnp.zeros((16, out_ch), F32)
-    gf[9 * ch :, :] = jnp.zeros((16, ch), F32)
-    for a in range(3):
-        turned = dot(cturn[...], hid[1, starts[a] : starts[a] + half].reshape(half * wide, 3 * ch))
-        for b in range(3):
-            at = (a * 3 + b) * ch
-            gd[at : at + ch, :] = turned[:, b * ch : (b + 1) * ch].T * mask_down
     pack(gd, send_d)
     swap_d = remote(send_d.at[1 - core], other_d, swap_s.at[0], swap_r.at[0], mate)
     swap_d.start()
@@ -475,6 +515,9 @@
                 S((rows, 2 * ch), F32),
                 S((rows, 2 * ch), F32),
                 S((8, 2 * ch), F32),
+                S((2, wide, 3 * ch), BF16),
+                S((2, half, wide, out_ch), F32),
+                S((2, half, out_ch), F32),
                 S((half + 1, wide, 2 * out_ch), BF16),
                 S((half, out_ch), F32),
                 S((half, out_ch), F32),

time: 67.7 us -> 65.8 us (0.972)
  Pallas kernels: 63.5 us -> 61.6 us
    pallas_call x1, Pallas kernels: 63.5 us -> 61.6 us  [local(): pl.pallas_call(functools.partial(kernel, nlat, nlon, chunk, padded), out_...]
where the time goes in v2:
time: 65.8 us; the launch traced here: 65.6 us
  Pallas kernels  61.6 us (94%)
  local copies, waits for them, and re-layouts  3.29 us (5%)
    pallas_call x1, Pallas kernels, local(): pl.pallas_call(functools.partial(kernel, nlat, nlon, chunk, padded), out_...  61.6 us
    unnamed x7, local copies, waits for them, and re-layouts  3.29 us

profile of v2, /device:TPU:0, one launch (start us, length us, event | category | flops | bytes accessed | tf_op | source)
XLA Modules:
  0.0 65.6 jit_solution(6864197919437239403)
XLA Ops:
  0.6 61.6 %shard_map.121 = (bf16[16,64,256]{2,1,0:T(8,128)(2,1)}, f32[36,128]{1,0:T(8,128)}, f32[36,256]{1,0:T(8,128)}) custom-call(bf16[32,128,128]{2,1,0:T(8,128)(2,1)} %field.1, bf16[3,3,128,128]{3,2,1,0:T(8,128)(2,1)} %w_first.1, bf16[3,3,128,256]{3,2,1,0:T(8,128)(2,1)} %w_down.1, s32[128,128]{1,0:T(8,128)} %keep_first.1, s32[1,128]{1,0:T(1,128)} %bitcast.6, ...), custom_call_target="tpu_custom_call" | custom-call | tf_op jit(solution)/shard_map/pallas_call | solution.py:500
  62.3 0.0 copy-start.1
  62.3 1.9 %copy.16 = bf16[16,64,256]{2,1,0:T(8,128)(2,1)} copy(bf16[16,64,256]{2,1,0:T(8,128)(2,1)} %get-tuple-element.6) | data formatting | bytes 1048576
  64.2 0.0 copy-done.1
  64.2 0.0 copy-start
  64.2 0.6 copy.17
  64.8 0.2 copy-done
  65.0 0.6 copy.18
Async XLA Ops:
  62.3 1.9 %copy-start.1 = (f32[36,128]{1,0:T(8,128)S(1)}, f32[36,128]{1,0:T(8,128)}, u32[]{:S(2)}) copy-start(f32[36,128]{1,0:T(8,128)} %get-tuple-element.7) | copy-start | bytes 55300
  64.2 0.8 %copy-start = (f32[36,256]{1,0:T(8,128)S(1)}, f32[36,256]{1,0:T(8,128)}, u32[]{:S(2)}) copy-start(f32[36,256]{1,0:T(8,128)} %get-tuple-element.8) | copy-start | bytes 110596

commit v3 on v2

--- a/solution.py
+++ b/solution.py
@@ -14,7 +14,7 @@
 F32 = jnp.float32
 BF16 = jnp.bfloat16
 HIGH = lax.Precision.HIGHEST
-BLOCK = 8
+BLOCK = 16
 
 
 def dot(a, b):
@@ -351,6 +351,51 @@
         for b in range(3):
             at = (a * 3 + b) * ch
             gd[at : at + ch, :] = turned[:, b * ch : (b + 1) * ch].T * mask_down
+    pairs = devices // 2
+    core = lax.rem(lon, 2)
+    mine = me // 2
+    mate = (lat, lon + 1 - 2 * core)
+
+    def pack(grads, buffer):
+        for d in range(devices):
+            buffer[d % 2, d // 2] = grads[d * chunk : d * chunk + padded, :].astype(BF16)
+
+    def merge(buffer, other, merged, got):
+        def one_chunk(h, carry):
+            merged[h] = (buffer[core, h].astype(F32) + other[h].astype(F32)).astype(BF16)
+            return carry
+
+        lax.fori_loop(0, pairs, one_chunk, 0)
+        got[mine] = merged[mine]
+
+    def scatter(merged, got, ssem, rsem):
+        def owner(h):
+            return place(2 * h + core)
+
+        def start(k, carry):
+            to = lax.rem(mine + k, pairs)
+            remote(merged.at[to], got.at[mine], ssem.at[k], rsem.at[k], owner(to)).start()
+            return carry
+
+        def receive(k, carry):
+            at = lax.rem(mine + pairs - k, pairs)
+            remote(merged.at[at], got.at[at], ssem.at[k], rsem.at[k], owner(at)).wait_recv()
+            return carry
+
+        def sent(k, carry):
+            to = lax.rem(mine + k, pairs)
+            remote(merged.at[to], got.at[mine], ssem.at[k], rsem.at[k], owner(to)).wait_send()
+            return carry
+
+        return (
+            lambda: lax.fori_loop(1, pairs, start, 0),
+            lambda: lax.fori_loop(1, pairs, receive, 0),
+            lambda: lax.fori_loop(1, pairs, sent, 0),
+        )
+
+    pack(gd, send_d)
+    swap_d = remote(send_d.at[1 - core], other_d, swap_s.at[0], swap_r.at[0], mate)
+    swap_d.start()
     finish_sends(cots)
     finish_receives(cots)
     bottom = lax.broadcasted_iota(jnp.int32, (16, out_ch), 0) == 15
@@ -389,53 +434,11 @@
     go, receive_b, sent_b = everyone(lambda to: stat_b.at[me], stat_b, sb_s, sb_r)
     go()
 
-    pairs = devices // 2
-    core = lax.rem(lon, 2)
-    mine = me // 2
-    mate = (lat, lon + 1 - 2 * core)
-
-    def pack(grads, buffer):
-        for d in range(devices):
-            buffer[d % 2, d // 2] = grads[d * chunk : d * chunk + padded, :].astype(BF16)
-
-    def merge(buffer, other, merged, got):
-        def one_chunk(h, carry):
-            merged[h] = (buffer[core, h].astype(F32) + other[h].astype(F32)).astype(BF16)
-            return carry
-
-        lax.fori_loop(0, pairs, one_chunk, 0)
-        got[mine] = merged[mine]
-
-    def scatter(merged, got, ssem, rsem):
-        def owner(h):
-            return place(2 * h + core)
-
-        def start(k, carry):
-            to = lax.rem(mine + k, pairs)
-            remote(merged.at[to], got.at[mine], ssem.at[k], rsem.at[k], owner(to)).start()
-            return carry
-
-        def receive(k, carry):
-            at = lax.rem(mine + pairs - k, pairs)
-            remote(merged.at[at], got.at[at], ssem.at[k], rsem.at[k], owner(at)).wait_recv()
-            return carry
-
-        def sent(k, carry):
-            to = lax.rem(mine + k, pairs)
-            remote(merged.at[to], got.at[mine], ssem.at[k], rsem.at[k], owner(to)).wait_send()
-            return carry
-
-        return (
-            lambda: lax.fori_loop(1, pairs, start, 0),
-            lambda: lax.fori_loop(1, pairs, receive, 0),
-            lambda: lax.fori_loop(1, pairs, sent, 0),
-        )
-
-    pack(gd, send_d)
-    swap_d = remote(send_d.at[1 - core], other_d, swap_s.at[0], swap_r.at[0], mate)
-    swap_d.start()
     go_d, receive_d, sent_d = scatter(merged_d, got_d, rd_s, rd_r)
 
+    swap_d.wait_recv()
+    merge(send_d, other_d, merged_d, got_d)
+    go_d()
     receive_b()
     back = grouped(jnp.sum(stat_b[...], axis=0)) / count
     m1, m2 = back[0:1], back[1:2]
@@ -447,9 +450,6 @@
                 value = ghat[e, r : r + BLOCK, :, p * ch : (p + 1) * ch].reshape(size, ch)
                 gpre = inv_s * (value - m1 - hat * m2)
                 gturn[e, p * ch : (p + 1) * ch, step * size : (step + 1) * size] = gpre.T.astype(BF16)
-    swap_d.wait_recv()
-    merge(send_d, other_d, merged_d, got_d)
-    go_d()
     for a in range(3):
         acc = None
         for e in range(2):

time: 65.8 us -> 61.6 us (0.936)
  Pallas kernels: 61.6 us -> 57.5 us
    pallas_call x1, Pallas kernels: 61.6 us -> 57.5 us  [local(): pl.pallas_call(functools.partial(kernel, nlat, nlon, chunk, padded), out_...]
where the time goes in v3:
time: 61.6 us; the launch traced here: 61.4 us
  Pallas kernels  57.5 us (93%)
  local copies, waits for them, and re-layouts  3.29 us (5%)
  between operations  0.65 us (1%)
    pallas_call x1, Pallas kernels, local(): pl.pallas_call(functools.partial(kernel, nlat, nlon, chunk, padded), out_...  57.5 us
    unnamed x7, local copies, waits for them, and re-layouts  3.29 us

profile of v3, /device:TPU:0, one launch (start us, length us, event | category | flops | bytes accessed | tf_op | source)
XLA Modules:
  0.0 61.4 jit_solution(508256117943829947)
XLA Ops:
  0.6 57.5 %shard_map.121 = (bf16[16,64,256]{2,1,0:T(8,128)(2,1)}, f32[36,128]{1,0:T(8,128)}, f32[36,256]{1,0:T(8,128)}) custom-call(bf16[32,128,128]{2,1,0:T(8,128)(2,1)} %field.1, bf16[3,3,128,128]{3,2,1,0:T(8,128)(2,1)} %w_first.1, bf16[3,3,128,256]{3,2,1,0:T(8,128)(2,1)} %w_down.1, s32[128,128]{1,0:T(8,128)} %keep_first.1, s32[1,128]{1,0:T(1,128)} %bitcast.6, ...), custom_call_target="tpu_custom_call" | custom-call | tf_op jit(solution)/shard_map/pallas_call | solution.py:500
  58.1 0.0 copy-start.1
  58.1 1.9 %copy.16 = bf16[16,64,256]{2,1,0:T(8,128)(2,1)} copy(bf16[16,64,256]{2,1,0:T(8,128)(2,1)} %get-tuple-element.6) | data formatting | bytes 1048576
  60.0 0.0 copy-done.1
  60.0 0.0 copy-start
  60.0 0.6 copy.17
  60.6 0.2 copy-done
  60.8 0.6 %copy.18 = f32[36,256]{1,0:T(8,128)} copy(f32[36,256]{1,0:T(8,128)S(1)} %copy-done) | data formatting | bytes 73728
Async XLA Ops:
  58.1 1.9 %copy-start.1 = (f32[36,128]{1,0:T(8,128)S(1)}, f32[36,128]{1,0:T(8,128)}, u32[]{:S(2)}) copy-start(f32[36,128]{1,0:T(8,128)} %get-tuple-element.7) | copy-start | bytes 55300
  60.0 0.8 %copy-start = (f32[36,256]{1,0:T(8,128)S(1)}, f32[36,256]{1,0:T(8,128)}, u32[]{:S(2)}) copy-start(f32[36,256]{1,0:T(8,128)} %get-tuple-element.8) | copy-start | bytes 110596

commit v4 on v3

--- a/solution.py
+++ b/solution.py
@@ -471,11 +471,11 @@
 
         return lax.fori_loop(0, pairs, add, jnp.zeros((padded, width), F32))[:chunk]
 
+    receive_d()
+    gdown_ref[...] = add_up(got_d, out_ch)
     swap_f.wait_recv()
     merge(send_f, other_f, merged_f, got_f)
     go_f()
-    receive_d()
-    gdown_ref[...] = add_up(got_d, out_ch)
     receive_f()
     gfirst_ref[...] = add_up(got_f, ch)
     sent_b()

time: 61.6 us -> 62.6 us (1.016)
  Pallas kernels: 57.5 us -> 58.4 us
    pallas_call x1, Pallas kernels: 57.5 us -> 58.4 us  [local(): pl.pallas_call(functools.partial(kernel, nlat, nlon, chunk, padded), out_...]
where the time goes in v4:
time: 62.6 us; the launch traced here: 62.3 us
  Pallas kernels  58.4 us (93%)
  local copies, waits for them, and re-layouts  3.29 us (5%)
  between operations  0.65 us (1%)
    pallas_call x1, Pallas kernels, local(): pl.pallas_call(functools.partial(kernel, nlat, nlon, chunk, padded), out_...  58.4 us
    unnamed x7, local copies, waits for them, and re-layouts  3.29 us

profile of v4, /device:TPU:0, one launch (start us, length us, event | category | flops | bytes accessed | tf_op | source)
XLA Modules:
  0.0 62.3 jit_solution(9740546752199472843)
XLA Ops:
  0.6 58.4 %shard_map.121 = (bf16[16,64,256]{2,1,0:T(8,128)(2,1)}, f32[36,128]{1,0:T(8,128)}, f32[36,256]{1,0:T(8,128)}) custom-call(bf16[32,128,128]{2,1,0:T(8,128)(2,1)} %field.1, bf16[3,3,128,128]{3,2,1,0:T(8,128)(2,1)} %w_first.1, bf16[3,3,128,256]{3,2,1,0:T(8,128)(2,1)} %w_down.1, s32[128,128]{1,0:T(8,128)} %keep_first.1, s32[1,128]{1,0:T(1,128)} %bitcast.6, ...), custom_call_target="tpu_custom_call" | custom-call | tf_op jit(solution)/shard_map/pallas_call | solution.py:500
  59.0 0.0 copy-start.1
  59.0 1.9 %copy.16 = bf16[16,64,256]{2,1,0:T(8,128)(2,1)} copy(bf16[16,64,256]{2,1,0:T(8,128)(2,1)} %get-tuple-element.6) | data formatting | bytes 1048576
  60.9 0.0 copy-done.1
  60.9 0.0 copy-start
  60.9 0.6 copy.17
  61.5 0.2 copy-done
  61.7 0.6 copy.18
Async XLA Ops:
  59.0 1.9 %copy-start.1 = (f32[36,128]{1,0:T(8,128)S(1)}, f32[36,128]{1,0:T(8,128)}, u32[]{:S(2)}) copy-start(f32[36,128]{1,0:T(8,128)} %get-tuple-element.7) | copy-start | bytes 55300
  60.9 0.8 %copy-start = (f32[36,256]{1,0:T(8,128)S(1)}, f32[36,256]{1,0:T(8,128)}, u32[]{:S(2)}) copy-start(f32[36,256]{1,0:T(8,128)} %get-tuple-element.8) | copy-start | bytes 110596
